TPU v7x, 128 devices: a whole 4x4x4 slice. The times are simulated.
128 devices in a mesh: section: 2 (over core), dp: 16 (over x, z), tensor: 4 (over y).
Axes of the slice: x: 4, y: 4, z: 4, core: 2. Of those that a mesh axis runs over, the one named last changes fastest.
Arguments:
- activations: float32 [2, 8192, 1024], P(None, ('dp', 'tensor')), may hold values from -6 to 6
- cotangent: float32 [2, 8192, 1024], P(None, ('dp', 'tensor')), may hold values from -6 to 6
- lengths: int32 [2, 16, 2], P(None, 'dp'), may hold values from 0 to 512, as said below
- norm_gain: float32 [2, 1024], P('section'), may hold values from 0.5 to 1.5
- in_weight: bfloat16 [2, 1024, 2, 2048], P('section', 'dp', None, 'tensor'), may hold values from -0.1875 to 0.1875
- bc_weight: bfloat16 [2, 1024, 256], P('section', 'dp'), may hold values from -0.1875 to 0.1875
- dt_weight: bfloat16 [2, 1024, 32], P('section', 'dp', 'tensor'), may hold values from -0.1875 to 0.1875
- conv_weight: float32 [2, 4, 2304], P('section'), may hold values from -3 to 3
- conv_bias: float32 [2, 2304], P('section'), may hold values from -3 to 3
- dt_bias: float32 [2, 32], P('section'), may hold values from -7 to -4
- a_log: float32 [2, 32], P('section'), may hold values from 0 to 3
- d_skip: float32 [2, 32], P('section'), may hold values from 0.5 to 1.5
- gated_gain: float32 [2, 2048], P('section'), may hold values from 0.5 to 1.5
- out_weight: bfloat16 [2, 2048, 1024], P('section', 'tensor', 'dp'), may hold values from -0.125 to 0.125
Outputs:
- layer_out: float32 [2, 2, 8192, 1024], P('section', None, ('dp', 'tensor'))
- layer_grad: float32 [2, 2, 8192, 1024], P('section', None, ('dp', 'tensor'))
- norm_gain_grad: float32 [2, 1024], P('section')
- in_weight_grad: float32 [2, 1024, 2, 2048], P('section', 'dp', None, 'tensor')
- bc_weight_grad: float32 [2, 1024, 256], P('section', ('dp', 'tensor'))
- dt_weight_grad: float32 [2, 1024, 32], P('section', 'dp', 'tensor')
- conv_weight_grad: float32 [2, 4, 2304], P('section')
- conv_bias_grad: float32 [2, 2304], P('section')
- dt_bias_grad: float32 [2, 32], P('section')
- a_log_grad: float32 [2, 32], P('section')
- d_skip_grad: float32 [2, 32], P('section')
- gated_gain_grad: float32 [2, 2048], P('section')
- out_weight_grad: float32 [2, 2048, 1024], P('section', 'tensor', 'dp')
Inputs may be any that keep to these rules, and one draw needn't show every extreme that they name: lengths[m, g, 0] is over 384 and the two lengths of a group sum to at most 512; in every micro-batch one group has lengths[m, g, 0] = 512; slots past the two sequences are padding.
All inputs are finite; a program needn't handle non-finite values.
Results may differ from a plain program's by a relative error of at most 0.025.
Values may be sent and summed in bfloat16 or wider, within the bound.
A program may use at most 192 MiB of HBM per device.

v0:
```python
import functools

import jax
import jax.numpy as jnp
from jax import lax
from jax.experimental import pallas as pl
from jax.experimental.pallas import tpu as pltpu
from jax.sharding import PartitionSpec as P

D = 1024
DI = 2048
H = 32
N = 128
CONV = 4
T = 512
ROWS = 128
CH = 512
HL = 8
WZX = 1024
WP = 1408
WALL = 1920
NDP = 16
EPSILON = 1e-05
LOG2E = 1.4426950408889634
NEG = -1e30
F32 = jnp.float32
BF16 = jnp.bfloat16
MESH = pl.DeviceIdType.MESH
VM = pltpu.VMEM
FWD_VMEM = 12 << 20
BWD_VMEM = 16 << 20


def dot_nn(a, b):
    return lax.dot_general(a, b, (((1,), (0,)), ((), ())), preferred_element_type=F32)


def dot_nt(a, b):
    return lax.dot_general(a, b, (((1,), (1,)), ((), ())), preferred_element_type=F32)


def dot_tn(a, b):
    return lax.dot_general(a, b, (((0,), (0,)), ((), ())), preferred_element_type=F32)


def pieces(v, count):
    parts = []
    for _ in range(count):
        part = v.astype(BF16)
        parts.append(part)
        v = v - part.astype(F32)
    return parts


def sum_rows_nt(selector, v, count):
    return sum(dot_nt(selector, part) for part in pieces(v, count))


def rows_times(v, matrix):
    a, b, c = pieces(v, 3)
    stacked = jnp.concatenate([a.astype(F32), b.astype(F32), c.astype(F32), jnp.zeros_like(v)], 0)
    out = dot_nn(stacked.astype(BF16), matrix)
    return out[0:8] + out[8:16] + out[16:24]


def iota(shape, dim):
    return lax.broadcasted_iota(jnp.int32, shape, dim)


def segment_of(position, e0, e1):
    return (position >= e0).astype(jnp.int32) + (position >= e1).astype(jnp.int32)


def conv_masks(e0, e1):
    p = iota((T, 128), 0)
    seg = segment_of(p, e0, e1)
    return [
        jnp.where((p >= k) & (segment_of(p - k, e0, e1) == seg), 1.0, 0.0).astype(F32)
        for k in range(1, CONV)
    ]


def conv_pre(v, masks, cw, lanes):
    pre = cw[CONV : CONV + 1, lanes] + cw[CONV - 1 : CONV, lanes] * v
    for k in range(1, CONV):
        pre = pre + cw[CONV - 1 - k : CONV - k, lanes] * (masks[k - 1] * pltpu.roll(v, k, 0))
    return pre


def sigmoid(v):
    return 0.5 * jnp.tanh(0.5 * v) + 0.5


def steps_of(dt_tile, hp_ref):
    raw = jnp.transpose(dt_tile)[0:HL] + hp_ref[:, 0:1]
    step = jnp.maximum(raw, 0.0) + jnp.log1p(jnp.exp(-jnp.abs(raw)))
    rate = hp_ref[:, 1:2]
    upper = jnp.where(iota((T, T), 0) <= iota((T, T), 1), 1.0, 0.0).astype(BF16)
    cum = rows_times(step * rate, upper) * LOG2E
    columns = jnp.transpose(
        jnp.concatenate([cum, step, jnp.zeros((112, T), F32)], axis=0)
    )
    return raw, step, cum, columns


def pair_columns(columns, first, j, rows=T):
    low = iota((rows, 128), 1) < 64
    return jnp.where(
        low,
        jnp.broadcast_to(columns[:, first + 2 * j : first + 2 * j + 1], (rows, 128)),
        jnp.broadcast_to(columns[:, first + 2 * j + 1 : first + 2 * j + 2], (rows, 128)),
    )


def tile(j):
    return slice(128 * j, 128 * j + 128)


def layer_params(par, layer):
    return (
        par.at[layer, :, pl.ds(0, 768)],
        par.at[layer, :, pl.ds(768, 128)],
        par.at[layer, :, pl.ds(896, 512)],
    )


def skip_row(hp, j):
    low = iota((1, 128), 1) < 64
    first = jnp.broadcast_to(hp[2 * j : 2 * j + 1, 2:3], (1, 128))
    second = jnp.broadcast_to(hp[2 * j + 1 : 2 * j + 2, 2:3], (1, 128))
    return jnp.where(low, first, second)


def segment_ends(lengths):
    c = lax.axis_index("section")
    first = lengths[c, 0, 0]
    return first, first + lengths[c, 0, 1]


def project(hid, w, proj):
    tokens = hid[...].reshape(T, D)
    for first, width in ((0, 512), (512, 512), (1024, 384)):
        at = slice(first, first + width)
        proj[:, at] = dot_nn(tokens, w[:, :, :, at].reshape(D, width))


def scale_back(db, w, d_scaled):
    d_scaled[...] = dot_nn(db[...].reshape(T, D), w[:, :, :, WP:WALL].reshape(D, CH))


def mixer_fwd_kernel(layer, lens, par, hid, w, *rest, early=None):
    with_grad = layer == 1
    if with_grad:
        db, proj, kept, part, yssd, coef, d_scaled, gg, inn, xb, bb, cb, cumr, colr, *rest = rest
        st, buf, send_sems, recv_sems = rest
        me = Peers()
        barrier_start(me.ts)
        scale_back(db, w, d_scaled)
    else:
        proj, kept, part, yssd, st, gg, inn, xb, bb, cb, cumr, colr = rest
    cw, hp, rows = layer_params(par, layer)
    project(hid, w, proj)
    if early is not None:
        early()
    e0, e1 = segment_ends(lens)
    masks = conv_masks(e0, e1)
    _, _, cum, columns = steps_of(proj[:, 1280:1408], hp)
    cumr[...] = cum
    colr[...] = columns
    for j in range(4):
        v = proj[:, 512 + 128 * j : 640 + 128 * j]
        pre = conv_pre(v, masks, cw, tile(j))
        kept[:, tile(j)] = pre
        act = pre * sigmoid(pre)
        inn[:, tile(j)] = act
        xb[:, tile(j)] = (act * pair_columns(columns, HL, j)).astype(BF16)
    for j, ref in ((0, bb), (1, cb)):
        lanes = slice(512 + 128 * j, 640 + 128 * j)
        pre = conv_pre(proj[:, 1024 + 128 * j : 1152 + 128 * j], masks, cw, lanes)
        kept[:, lanes] = pre
        ref[...] = (pre * sigmoid(pre)).astype(BF16)
    low = iota((128, 128), 1) < 64
    for i in range(4):
        n = 128 * (i + 1)
        here = slice(128 * i, n)
        scores = dot_nt(cb[here, :], bb[0:n, :])
        p = iota((128, n), 0) + 128 * i
        q = iota((128, n), 1)
        bias = jnp.where((p >= q) & (segment_of(p, e0, e1) == segment_of(q, e0, e1)), 0.0, NEG).astype(F32)
        for j in range(4):
            mixing = []
            for h in (2 * j, 2 * j + 1):
                decay = jnp.exp2(colr[here, h : h + 1] - cumr[h : h + 1, 0:n] + bias)
                mixing.append((scores * decay).astype(BF16))
            both = dot_nn(jnp.concatenate(mixing, axis=0), xb[0:n, tile(j)])
            yssd[here, tile(j)] = jnp.where(low, both[0:128], both[128:256])
    squares = jnp.zeros((8, T), F32)
    dots = jnp.zeros((8, T), F32)
    ones = jnp.ones((8, 128), BF16)
    for j in range(4):
        z = proj[:, tile(j)]
        gated = (yssd[:, tile(j)] + skip_row(hp, j) * inn[:, tile(j)]) * (z * sigmoid(z))
        gained = gated * rows[0:1, tile(j)]
        gg[:, tile(j)] = gained.astype(BF16)
        squares = squares + sum_rows_nt(ones, gated * gated, 1)
        if with_grad:
            dots = dots + sum_rows_nt(ones, gained * d_scaled[:, tile(j)], 2)
    row = iota((8, T), 0)
    both = jnp.where(row == 0, squares, jnp.where(row == 1, dots, 0.0))
    for i in range(4):
        st[i] = both[:, tile(i)]
    if with_grad:
        exchange = stats_exchange(Link(send_sems, recv_sems), st, buf, coef, me)
        next(exchange)
    for x in range(4):
        columns_out = slice(256 * x, 256 * x + 256)
        branch = dot_nt(gg[...], w[x, :, :, WP:WALL].reshape(256, CH)).astype(BF16)
        part[:, :, columns_out] = branch.reshape(4, ROWS, 256)
    if with_grad:
        run(exchange)


def vmem_specs(count):
    return [pl.BlockSpec(memory_space=VM)] * count


def fwd_scratch():
    return [
        VM((T, CH), BF16),
        VM((T, CH), F32),
        VM((T, CH), BF16),
        VM((T, N), BF16),
        VM((T, N), BF16),
        VM((8, T), F32),
        VM((T, 128), F32),
    ]


def mixer_fwd(layer, lens, par, hid, w, *db):
    out_shape = [
        jax.ShapeDtypeStruct((T, WP), F32),
        jax.ShapeDtypeStruct((T, 768), F32),
        jax.ShapeDtypeStruct((4, ROWS, D), BF16),
        jax.ShapeDtypeStruct((T, CH), F32),
        jax.ShapeDtypeStruct((4, 8, 128), F32),
    ] + [jax.ShapeDtypeStruct((T, CH), F32)] * layer
    shared = {"collective_id": 2, "has_side_effects": True} if layer else {}
    return pl.pallas_call(
        functools.partial(mixer_fwd_kernel, layer),
        out_shape=tuple(out_shape),
        in_specs=[pl.BlockSpec(memory_space=pltpu.SMEM)] + vmem_specs(3 + len(db)),
        out_specs=tuple(vmem_specs(len(out_shape))),
        scratch_shapes=fwd_scratch() + ([VM((4, 8, 128), F32), VM((4, 4, 8, 128), F32)] + link_scratch(3)) * layer,
        compiler_params=pltpu.CompilerParams(vmem_limit_bytes=FWD_VMEM, **shared),
        name="mixer_fwd",
    )(lens, par, hid, w, *db)


def head_selector(j):
    head = 2 * j + (iota((8, 128), 1) >= 64).astype(jnp.int32)
    return jnp.where(iota((8, 128), 0) == head, 1.0, 0.0).astype(BF16)


def back_roll(v, k):
    return pltpu.roll(v, T - k, 0)


def conv_back(d_pre, v, masks, cw, lanes, sums, column0):
    d_v = cw[CONV - 1 : CONV, lanes] * d_pre
    out = slice(column0, column0 + 128)
    sums[CONV : CONV + 1, out] = jnp.sum(d_pre, axis=0, keepdims=True)
    sums[CONV - 1 : CONV, out] = jnp.sum(d_pre * v, axis=0, keepdims=True)
    for k in range(1, CONV):
        masked = masks[k - 1] * d_pre
        d_v = d_v + cw[CONV - 1 - k : CONV - k, lanes] * back_roll(masked, k)
        sums[CONV - 1 - k : CONV - k, out] = jnp.sum(masked * pltpu.roll(v, k, 0), axis=0, keepdims=True)
    return d_v


def mixer_bwd_kernel(layer, lens, par, w, proj, kept, yssd, coef, *rest, early=None, later=None):
    given, *rest = rest
    dh, d_proj, scaled, sums, heads, inn, xb, dyb, dyf, dx, bb, cb, d_c, cumr, colr, *rest = rest
    if layer == 1:
        d_scaled = given
    else:
        db, d_scaled = given, rest[0]
        scale_back(db, w, d_scaled)
    cw, hp, rows = layer_params(par, layer)
    e0, e1 = segment_ends(lens)
    masks = conv_masks(e0, e1)
    raw, step, cum, columns = steps_of(proj[:, 1280:1408], hp)
    cumr[...] = cum
    colr[...] = columns
    norm_cols = jnp.transpose(jnp.concatenate(
        [jnp.concatenate([coef[i] for i in range(4)], axis=1), jnp.zeros((120, T), F32)], axis=0
    ))
    s_col = jnp.broadcast_to(norm_cols[:, 0:1], (T, 128))
    k_col = jnp.broadcast_to(norm_cols[:, 1:2], (T, 128))
    sums[...] = jnp.zeros_like(sums)
    d_skip = jnp.zeros((8, T), F32)
    for j in range(4):
        selector = head_selector(j)
        pre = kept[:, tile(j)]
        act = pre * sigmoid(pre)
        inn[:, tile(j)] = act
        xb[:, tile(j)] = (act * pair_columns(columns, HL, j)).astype(BF16)
        z = proj[:, tile(j)]
        sig = sigmoid(z)
        gate = z * sig
        y = yssd[:, tile(j)] + skip_row(hp, j) * act
        gated = y * gate
        gs = gated * s_col
        gain = rows[0:1, tile(j)]
        dsc = d_scaled[:, tile(j)]
        scaled[:, tile(j)] = (gs * gain).astype(BF16)
        sums[5:6, tile(j)] = jnp.sum(gs * dsc, axis=0, keepdims=True)
        d_gated = s_col * gain * dsc - gated * k_col
        d_proj[:, tile(j)] = (d_gated * y * (sig * (1.0 + z * (1.0 - sig)))).astype(BF16)
        dy = d_gated * gate
        dyf[:, tile(j)] = dy
        dyb[:, tile(j)] = dy.astype(BF16)
        d_skip = d_skip + sum_rows_nt(selector, dy * act, 2)
    for j, ref in ((0, bb), (1, cb)):
        pre = kept[:, 512 + 128 * j : 640 + 128 * j]
        ref[...] = (pre * sigmoid(pre)).astype(BF16)
    if early is not None:
        early()
    d_c[...] = jnp.zeros_like(d_c)
    low = iota((128, 128), 1) < 64
    zero = jnp.zeros((128, 128), BF16)
    d_b_blocks = []
    for i in range(4):
        first = 128 * i
        n = T - first
        here = slice(first, first + 128)
        scores = dot_nt(bb[here, :], cb[first:T, :])
        q = iota((128, n), 0) + first
        p = iota((128, n), 1) + first
        bias = jnp.where((p >= q) & (segment_of(p, e0, e1) == segment_of(q, e0, e1)), 0.0, NEG).astype(F32)
        d_scores = jnp.zeros((128, n), F32)
        for j in range(4):
            x_tile = xb[here, tile(j)]
            dy_tile = dyb[first:T, tile(j)]
            heads_of = jnp.concatenate([jnp.where(low, x_tile, zero), jnp.where(low, zero, x_tile)], axis=0)
            d_mixing = dot_nt(heads_of, dy_tile)
            mixing = []
            for k in (0, 1):
                h = 2 * j + k
                decay = jnp.exp2(cumr[h : h + 1, first:T] - colr[here, h : h + 1] + bias)
                mixing.append((scores * decay).astype(BF16))
                d_scores = d_scores + d_mixing[128 * k : 128 * k + 128] * decay
            both = dot_nn(jnp.concatenate(mixing, axis=0), dy_tile)
            dx[here, tile(j)] = jnp.where(low, both[0:128], both[128:256])
        d_scores = d_scores.astype(BF16)
        d_b_blocks.append(dot_nn(d_scores, cb[first:T, :]))
        d_c[first:T, :] = d_c[first:T, :] + dot_tn(d_scores, bb[here, :])
    if later is not None:
        later()
    d_cum = jnp.zeros((8, T), F32)
    d_step = jnp.zeros((8, T), F32)
    for j in range(4):
        selector = head_selector(j)
        dxt = dx[:, tile(j)]
        act = inn[:, tile(j)]
        change = dyb[:, tile(j)].astype(F32) * yssd[:, tile(j)] - xb[:, tile(j)].astype(F32) * dxt
        d_cum = d_cum + sum_rows_nt(selector, change, 3)
        d_step = d_step + sum_rows_nt(selector, act * dxt, 2)
        d_act = pair_columns(columns, HL, j) * dxt + skip_row(hp, j) * dyf[:, tile(j)]
        v = proj[:, 512 + 128 * j : 640 + 128 * j]
        pre = kept[:, tile(j)]
        sig = sigmoid(pre)
        d_pre = d_act * (sig * (1.0 + pre * (1.0 - sig)))
        d_proj[:, 512 + 128 * j : 640 + 128 * j] = conv_back(d_pre, v, masks, cw, tile(j), sums, 128 * j).astype(BF16)
    for j in (0, 1):
        lanes = slice(512 + 128 * j, 640 + 128 * j)
        at = slice(1024 + 128 * j, 1152 + 128 * j)
        v = proj[:, at]
        pre = kept[:, lanes]
        sig = sigmoid(pre)
        d_act = jnp.concatenate(d_b_blocks, axis=0) if j == 0 else d_c[...]
        d_pre = d_act * (sig * (1.0 + pre * (1.0 - sig)))
        d_proj[:, at] = conv_back(d_pre, v, masks, cw, lanes, sums, 512 + 128 * j).astype(BF16)
    lower = jnp.where(iota((T, T), 0) >= iota((T, T), 1), 1.0, 0.0).astype(BF16)
    d_a = rows_times(d_cum, lower)
    rate = hp[:, 1:2]
    d_raw = (d_step + rate * d_a) * sigmoid(raw)
    d_proj[:, 1280:1408] = jnp.transpose(
        jnp.concatenate([d_raw, jnp.zeros((120, T), F32)], axis=0)
    ).astype(BF16)
    bias_grad = jnp.broadcast_to(jnp.sum(d_raw, axis=1, keepdims=True), (8, 128))
    rate_grad = jnp.broadcast_to(jnp.sum(d_a * step, axis=1, keepdims=True) * rate, (8, 128))
    skip_grad = jnp.broadcast_to(jnp.sum(d_skip, axis=1, keepdims=True), (8, 128))
    lane = iota((8, 128), 1)
    by_head = jnp.where(
        lane == 0, bias_grad, jnp.where(lane == 1, rate_grad, jnp.where(lane == 2, skip_grad, 0.0))
    )
    heads[...] = jnp.transpose(jnp.concatenate([by_head, jnp.zeros((120, 128), F32)], axis=0))[0:8]
    for x in range(4):
        back = dot_nt(d_proj[...], w[x, :, :, 0:WP].reshape(256, WP)).astype(BF16)
        dh[:, :, 256 * x : 256 * x + 256] = back.reshape(4, ROWS, 256)


def bwd_scratch():
    return [
        VM((4, ROWS, D), BF16),
        VM((T, WP), BF16),
        VM((T, CH), BF16),
    ], [
        VM((T, CH), F32),
        VM((T, CH), BF16),
        VM((T, CH), BF16),
        VM((T, CH), F32),
        VM((T, CH), F32),
        VM((T, N), BF16),
        VM((T, N), BF16),
        VM((T, N), F32),
        VM((8, T), F32),
        VM((T, 128), F32),
    ]


def places():
    section = lax.axis_index("section")
    dp = lax.axis_index("dp")
    return section, dp // 4, dp % 4, lax.axis_index("tensor")


class Peers:
    def __init__(self):
        self.c, self.x, self.z, self.t = places()
        self.core = {"section": 1 - self.c}
        self.xs = [{"dp": ((self.x + o) % 4) * 4 + self.z} for o in (1, 2, 3)]
        self.zs = [{"dp": self.x * 4 + (self.z + o) % 4} for o in (1, 2, 3)]
        self.ts = [{"tensor": (self.t + o) % 4} for o in (1, 2, 3)]
        self.far_ts = [{"section": 1 - self.c, "tensor": (self.t + o) % 4} for o in (1, 2, 3)]

    def near_dp(self):
        return [self.core] + self.xs + self.zs + self.ts

    def everyone(self):
        return [self.core] + self.xs + self.zs + self.ts + self.far_ts


def barrier_start(peers):
    barrier = pltpu.get_barrier_semaphore()
    for peer in peers:
        pl.semaphore_signal(barrier, inc=1, device_id=peer, device_id_type=MESH)


def barrier_end(peers):
    pl.semaphore_wait(pltpu.get_barrier_semaphore(), len(peers))


def greet(peers):
    barrier_start(peers)
    barrier_end(peers)


class Link:
    def __init__(self, send_sems, recv_sems):
        self.send_sems, self.recv_sems, self.sent = send_sems, recv_sems, []

    def send(self, src, dst, peer):
        k = len(self.sent)
        copy = pltpu.make_async_remote_copy(
            src_ref=src, dst_ref=dst, send_sem=self.send_sems.at[k], recv_sem=self.recv_sems.at[k],
            device_id=peer, device_id_type=MESH,
        )
        copy.start()
        self.sent.append(copy)
        return copy

    def drain(self):
        for copy in self.sent:
            copy.wait_send()


def spread(link, block, r, peers):
    plus, minus = peers[0], peers[2]

    def go(k, half, peer):
        return link.send(block(k, half), block(k, half), peer)

    from_left = [go(r, 0, plus)]
    from_right = [go(r, 1, minus)]
    from_left.append(go(r, 1, plus))
    from_right.append(go(r, 0, minus))
    yield
    from_left[0].wait_recv()
    far = [go((r + 3) % 4, 0, plus)]
    from_right[0].wait_recv()
    far.append(go((r + 1) % 4, 1, minus))
    yield
    for copy in (from_left[1], from_right[1]):
        copy.wait_recv()
    yield
    for copy in far:
        copy.wait_recv()
    yield


def collect(link, part, relay, sums, inbox, r, peers):
    plus, minus = peers[0], peers[2]
    left, right, far = (r + 3) % 4, (r + 1) % 4, (r + 2) % 4
    up = link.send(part(far, 0), relay.at[0], plus)
    down = link.send(part(far, 1), relay.at[1], minus)
    last = [
        link.send(part(right, 1), inbox(0, 1), plus),
        link.send(part(left, 0), inbox(1, 0), minus),
    ]
    yield
    up.wait_recv()
    sums[0] = (part(right, 0)[...].astype(F32) + relay[0].astype(F32)).astype(BF16)
    last.append(link.send(sums.at[0], inbox(0, 0), plus))
    down.wait_recv()
    sums[1] = (part(left, 1)[...].astype(F32) + relay[1].astype(F32)).astype(BF16)
    last.append(link.send(sums.at[1], inbox(1, 1), minus))
    yield
    for copy in last:
        copy.wait_recv()
    yield


def run(steps):
    for _ in steps:
        pass


def token_halves(ref):
    return lambda k, half: ref.at[k, pl.ds(64 * half, 64)]


def collect_tokens(link, ref, relay, sums, inbox, me):
    return collect(link, token_halves(ref), relay, sums, token_halves(inbox), me.t, me.ts)


def spread_tokens(link, ref, me):
    return spread(link, token_halves(ref), me.t, me.ts)


def core_rows(c):
    first = pl.multiple_of(32 * c, 32)
    return pl.ds(first, 32), pl.ds(first, 16), pl.ds(pl.multiple_of(32 * c + 16, 16), 16)


def gather_layer(link, own_sem, shard, w, me):
    c, x, z = me.c, me.x, me.z
    whole, a, b = core_rows(c)
    own = pltpu.make_async_copy(shard, w.at[x, z, whole], own_sem)
    own.start()
    first = []
    for o in range(3):
        first.append(link.send(shard.at[pl.ds(0, 16)], w.at[x, z, a], me.zs[o]))
        first.append(link.send(shard.at[pl.ds(16, 16)], w.at[x, z, b], me.xs[o]))
    yield
    own.wait()
    for copy in first:
        copy.wait_recv()
    along_x = spread(link, lambda k, half: w.at[k, pl.ds(2 * half, 2), a], x, me.xs)
    along_z = spread(link, lambda k, half: w.at[pl.ds(2 * half, 2), k, b], z, me.zs)
    next(along_x)
    next(along_z)
    core = []

    def to_core(o):
        block_a = w.at[(x + o) % 4, :, a]
        block_b = w.at[:, (z + o) % 4, b]
        core.append(link.send(block_a, block_a, me.core))
        core.append(link.send(block_b, block_b, me.core))

    to_core(0)
    yield
    next(along_x)
    next(along_z)
    yield
    next(along_x)
    next(along_z)
    to_core(1)
    to_core(3)
    yield
    next(along_x)
    next(along_z)
    to_core(2)
    yield
    for copy in core:
        copy.wait_recv()
    yield


GATHER_COPIES = 6 + 12 + 8


def reduce_rings(link, factors, grads, out_a, out_b, core_in, acc, relay, sums, inbox, me):
    c, x, z = me.c, me.x, me.z
    hid, d_proj, db, scaled = factors
    a, b = pl.ds(0, 16), pl.ds(16, 16)
    arrive = []
    for xx in range(4):
        at = slice(256 * xx, 256 * xx + 256)
        rows_in = dot_tn(hid[:, :, at].reshape(T, 256), d_proj[...]).astype(BF16)
        rows_out = dot_tn(db[:, :, at].reshape(T, 256), scaled[...]).astype(BF16)
        for k in range(8):
            block = slice(32 * k, 32 * k + 32)
            grads[k % 2, xx, k // 2, :, 0:WP] = rows_in[block]
            grads[k % 2, xx, k // 2, :, WP:WALL] = rows_out[block]
        arrive.append(link.send(grads.at[1 - c, xx], core_in.at[xx], me.core))
        if xx % 2 == 1:
            yield
    for xx in range(4):
        arrive[xx].wait_recv()
        acc[xx] = grads[c, xx] + core_in[xx]
    along_x = collect(
        link, lambda k, half: acc.at[k, pl.ds(2 * half, 2), a], relay.at[0], sums.at[0],
        lambda d, half: inbox.at[0, d, pl.ds(2 * half, 2)], x, me.xs,
    )
    next(along_x)
    along_z = collect(
        link, lambda k, half: acc.at[pl.ds(2 * half, 2), k, b], relay.at[1], sums.at[1],
        lambda d, half: inbox.at[1, d, pl.ds(2 * half, 2)], z, me.zs,
    )
    next(along_z)
    yield
    next(along_x)
    next(along_z)
    yield
    next(along_x)
    out_a[...] = (
        acc[x, :, a].astype(F32) + inbox[0, 0].astype(F32) + inbox[0, 1].astype(F32)
    ).astype(BF16)
    next(along_z)
    out_b[...] = (
        acc[:, z, b].astype(F32) + inbox[1, 0].astype(F32) + inbox[1, 1].astype(F32)
    ).astype(BF16)
    yield


RING_COPIES = 4 + 12


def reduce_last(link, sum_a, sum_b, out, bc_all, last_in, me):
    c, x, z = me.c, me.x, me.z
    last_a = [link.send(sum_a.at[(z + o + 1) % 4], last_in.at[0, o], me.zs[o]) for o in range(3)]
    last_b = [link.send(sum_b.at[(x + o + 1) % 4], last_in.at[1, o], me.xs[o]) for o in range(3)]
    yield
    rows, rows_a, rows_b = core_rows(c)
    for k, (copies, at, mine) in enumerate(((last_a, rows_a, sum_a.at[z]), (last_b, rows_b, sum_b.at[x]))):
        for copy in copies:
            copy.wait_recv()
        out[at, :] = (
            mine[...].astype(F32)
            + last_in[k, 0].astype(F32) + last_in[k, 1].astype(F32) + last_in[k, 2].astype(F32)
        )
    swap = [link.send(out.at[rows], out.at[rows], me.core)]

    def wanted(t):
        return pl.ds(pl.multiple_of(32 * c + 16 * (t % 2), 16), 16)

    bc_all[me.t, c] = out[wanted(me.t), 1024:1280]
    slot = bc_all.at[me.t, c]
    swap.append(link.send(slot, slot, me.core))
    for o in range(3):
        block = out.at[wanted(me.t + o + 1), pl.ds(1024, 256)]
        swap.append(link.send(block, slot, me.ts[o]))
        swap.append(link.send(block, slot, me.far_ts[o]))
    yield
    for copy in swap:
        copy.wait_recv()
    yield


LAST_COPIES = 6 + 8


def ring_scratch():
    return [
        VM((2, 4, 4, 32, WALL), BF16),
        VM((4, 4, 32, WALL), BF16), VM((4, 4, 32, WALL), BF16),
        VM((2, 2, 2, 16, WALL), BF16), VM((2, 2, 2, 16, WALL), BF16),
        VM((2, 2, 4, 16, WALL), BF16),
    ]


def last_scratch():
    return [VM((64, WALL), F32), VM((4, 2, 16, 2 * N), F32), VM((2, 3, 16, WALL), BF16)]


def token_scratch():
    return [VM((2, 64, D), BF16), VM((2, 64, D), BF16), VM((2, ROWS, D), BF16)]


def dma_sems(n):
    return pltpu.SemaphoreType.DMA((n,))


def link_scratch(*counts):
    return [pltpu.SemaphoreType.DMA((n,)) for n in counts for _ in range(2)]


def input_norm(u, gain):
    return u * lax.rsqrt(jnp.mean(u * u, axis=-1, keepdims=True) + EPSILON) * gain


def gain_of(par, layer):
    return par[layer, 0:1, 1408:2432]


def gather_kernel(
    lengths, w_in, w_bc, w_dt, w_out, conv_w, flat, u0, cot,
    w0, shard1, par, hid, db, valid,
    wsh, shards, turned, own_sem, g_s, g_r, e_s, e_r, h_s, h_r, d_s, d_r,
):
    me = Peers()
    c, t = me.c, me.t
    barrier_start(me.near_dp())
    wsh[:, 0:WZX] = w_in[...]
    wsh[:, 1024:1280] = w_bc[...]
    dt_rows = jnp.concatenate([w_dt[...].astype(F32), jnp.zeros((HL, 64), F32)], axis=1)
    dt_rows = jnp.concatenate([dt_rows, jnp.zeros((120, 128), F32)], axis=0)
    wsh[:, 1280:1408] = jnp.transpose(dt_rows)[0:64].astype(BF16)
    wsh[:, WP:WALL] = w_out[...]
    shards[c] = wsh[core_rows(c)[0], :]
    own = pl.ds(pl.multiple_of(CH * t, CH), CH)
    par[c] = jnp.zeros((8, 2432), F32)
    par[c, 0:4, 0:512] = conv_w[:, own]
    par[c, 0:4, 512:768] = conv_w[:, DI : DI + 2 * N]
    par[c, 4:5, 0:512] = flat[:, own]
    par[c, 4:5, 512:768] = flat[:, DI : DI + 2 * N]
    by_row = jnp.broadcast_to(flat[:, 5376:5504], (8, 128))
    row = iota((8, 128), 0)
    by_row = jnp.where(
        row == 0, by_row,
        jnp.where(row == 1, pltpu.roll(by_row, 128 - H, 1), pltpu.roll(by_row, 128 - 2 * H, 1)),
    )
    turned[...] = jnp.transpose(jnp.concatenate([by_row, jnp.zeros((120, 128), F32)], axis=0))
    heads = turned[pl.ds(pl.multiple_of(HL * t, HL), HL), :]
    par[c, :, 768:896] = jnp.where(iota((8, 128), 1) == 1, -jnp.exp(heads), heads)
    par[c, 0:1, 896:1408] = flat[:, pl.ds(pl.multiple_of(2304 + CH * t, 256), CH)]
    par[c, 0:1, 1408:2432] = flat[:, 4352:5376]
    end = lengths[c, 0, 0] + lengths[c, 0, 1]
    valid[...] = jnp.where(iota((ROWS, 128), 0) + ROWS * t < end, 1.0, 0.0).astype(F32)
    barrier_end(me.near_dp())
    early, weights = Link(e_s, e_r), Link(g_s, g_r)
    theirs = early.send(wsh.at[core_rows(1 - c)[0]], shards.at[c], me.core)
    par_copy = early.send(par.at[c], par.at[c], me.core)
    for j in range(8):
        db[t, :, tile(j)] = (cot[:, tile(j)] * valid[...]).astype(BF16)
    theirs.wait_recv()
    layer0 = gather_layer(weights, own_sem.at[0], shards.at[0], w0, me)
    next(layer0)
    par_copy.wait_recv()
    hid[t] = input_norm(u0[...], gain_of(par, 0)).astype(BF16)
    tokens, branch = Link(h_s, h_r), Link(d_s, d_r)
    hid_steps = spread_tokens(tokens, hid, me)
    db_steps = spread_tokens(branch, db, me)
    next(hid_steps)
    next(layer0)
    next(db_steps)
    next(layer0)
    next(hid_steps)
    shard1[...] = shards[1]
    next(layer0)
    next(db_steps)
    run(layer0)
    run(hid_steps)
    run(db_steps)
    for link in (early, weights, tokens, branch):
        link.drain()


def gather(*arrays):
    return pl.pallas_call(
        gather_kernel,
        out_shape=(
            jax.ShapeDtypeStruct((4, 4, 64, WALL), BF16),
            jax.ShapeDtypeStruct((32, WALL), BF16),
            jax.ShapeDtypeStruct((2, 8, 2432), F32),
            jax.ShapeDtypeStruct((4, ROWS, D), BF16),
            jax.ShapeDtypeStruct((4, ROWS, D), BF16),
            jax.ShapeDtypeStruct((ROWS, 128), F32),
        ),
        in_specs=[pl.BlockSpec(memory_space=pltpu.SMEM)] + vmem_specs(8),
        out_specs=tuple(vmem_specs(6)),
        scratch_shapes=[
            VM((64, WALL), BF16), VM((2, 32, WALL), BF16), VM((128, 128), F32),
            dma_sems(1),
        ]
        + link_scratch(GATHER_COPIES, 2, 6, 6),
        compiler_params=pltpu.CompilerParams(
            collective_id=0, has_side_effects=True, vmem_limit_bytes=6 << 20
        ),
        name="gather_weights",
    )(*arrays)


def column_of(row):
    return jnp.transpose(jnp.broadcast_to(row, (128, 128)))


def middle_kernel(
    lens, par, hid0, w0, u0, valid, shard1,
    proj, kept, yssd, total, u_next, s_out, hid, w1,
    part, st, gg, inn, xb, bb, cb, cumr, colr,
    relay, sums, inbox, sbuf, own_sem, g_s, g_r, p_s, p_r, b_s, b_r, h_s, h_r,
):
    me = Peers()
    t = me.t
    barrier_start(me.near_dp())
    weights, tokens, small, spreading = Link(g_s, g_r), Link(p_s, p_r), Link(b_s, b_r), Link(h_s, h_r)
    started = []

    def early():
        barrier_end(me.near_dp())
        started.append(gather_layer(weights, own_sem.at[0], shard1, w1, me))
        next(started[0])

    mixer_fwd_kernel(
        0, lens, par, hid0, w0, proj, kept, part, yssd, st, gg, inn, xb, bb, cb, cumr, colr, early=early
    )
    layer1 = started[0]
    sum_steps = collect_tokens(tokens, part, relay, sums, inbox, me)
    next(sum_steps)
    stats = [small.send(st.at[(t + o + 1) % 4], sbuf.at[o], me.ts[o]) for o in range(3)]
    next(layer1)
    next(sum_steps)
    for copy in stats:
        copy.wait_recv()
    s_row = lax.rsqrt((st[t] + sbuf[0] + sbuf[1] + sbuf[2]) / DI + EPSILON)
    s_out[...] = s_row
    scale = column_of(s_row[0:1]) * valid[...]
    next(layer1)
    run(sum_steps)
    total[...] = part[t].astype(F32) + inbox[0].astype(F32) + inbox[1].astype(F32)
    for j in range(8):
        u_next[:, tile(j)] = u0[:, tile(j)] + scale * total[:, tile(j)]
    hid[t] = input_norm(u_next[...], gain_of(par, 1)).astype(BF16)
    hid_steps = spread_tokens(spreading, hid, me)
    next(hid_steps)
    next(layer1)
    next(hid_steps)
    run(layer1)
    run(hid_steps)
    for link in (weights, tokens, small, spreading):
        link.drain()


def middle(*arrays):
    return pl.pallas_call(
        middle_kernel,
        out_shape=(
            jax.ShapeDtypeStruct((T, WP), F32),
            jax.ShapeDtypeStruct((T, 768), F32),
            jax.ShapeDtypeStruct((T, CH), F32),
            jax.ShapeDtypeStruct((ROWS, D), F32),
            jax.ShapeDtypeStruct((ROWS, D), F32),
            jax.ShapeDtypeStruct((8, 128), F32),
            jax.ShapeDtypeStruct((4, ROWS, D), BF16),
            jax.ShapeDtypeStruct((4, 4, 64, WALL), BF16),
        ),
        in_specs=[pl.BlockSpec(memory_space=pltpu.SMEM)] + vmem_specs(6),
        out_specs=tuple(vmem_specs(8)),
        scratch_shapes=[VM((4, ROWS, D), BF16), VM((4, 8, 128), F32)] + fwd_scratch() + token_scratch()
        + [VM((3, 8, 128), F32), pltpu.SemaphoreType.DMA((1,))]
        + link_scratch(GATHER_COPIES, 6, 3, 6),
        compiler_params=pltpu.CompilerParams(
            collective_id=1, has_side_effects=True, vmem_limit_bytes=16 << 20
        ),
        name="forward_0_and_tokens",
    )(*arrays)


def stats_exchange(link, st, buf, coef, me):
    barrier_end(me.ts)
    copies = [link.send(st, buf.at[me.t], peer) for peer in me.ts]
    buf[me.t] = st[...]
    yield
    for copy in copies:
        copy.wait_recv()
    for i in range(4):
        both = buf[0, i] + buf[1, i] + buf[2, i] + buf[3, i]
        s = lax.rsqrt(both[0:1] / DI + EPSILON)
        k = s * s * s * (both[1:2] / DI)
        row = iota((8, 128), 0)
        coef[i] = jnp.where(row == 0, s, jnp.where(row == 1, k, 0.0))
    link.drain()
    yield


def norm_back(u, gain, g, d_hidden):
    r = lax.rsqrt(jnp.mean(u * u, axis=-1, keepdims=True) + EPSILON)
    mean = jnp.mean(u * gain * d_hidden, axis=-1, keepdims=True)
    d_u = g + r * gain * d_hidden - u * (r * r * r) * mean
    return d_u, jnp.sum(u * r * d_hidden, axis=0, keepdims=True)


def back_middle_kernel(
    lens, par, w1, proj1, kept1, yssd1, coef1, d_scaled1, u, cot, valid, total0, s0, hid1, db1,
    sums1, heads1, g1, ng, db, coef, sum_a, sum_b,
    dh, d_proj1, scaled1, inn, xb, dyb, dyf, dx, bb, cb, d_c, cumr, colr,
    relay, sums, inbox, grads, core_in, acc, g_relay, g_sums, g_inbox,
    g_s, g_r, p_s, p_r, b_s, b_r, h_s, h_r,
):
    me = Peers()
    t = me.t
    barrier_start(me.near_dp())
    mixer_bwd_kernel(
        1, lens, par, w1, proj1, kept1, yssd1, coef1, d_scaled1, dh, d_proj1, scaled1, sums1, heads1,
        inn, xb, dyb, dyf, dx, bb, cb, d_c, cumr, colr,
        early=lambda: barrier_end(me.near_dp()),
    )
    weights, tokens, small, spreading = Link(g_s, g_r), Link(p_s, p_r), Link(b_s, b_r), Link(h_s, h_r)
    sum_steps = collect_tokens(tokens, dh, relay, sums, inbox, me)
    next(sum_steps)
    layer1 = reduce_rings(
        weights, (hid1, d_proj1, db1, scaled1), grads, sum_a, sum_b, core_in, acc,
        g_relay, g_sums, g_inbox, me,
    )
    next(layer1)
    next(sum_steps)
    next(layer1)
    next(layer1)
    run(sum_steps)
    total = dh[t].astype(F32) + inbox[0].astype(F32) + inbox[1].astype(F32)
    d_u, gain_term = norm_back(u[...], gain_of(par, 1), cot[...], total)
    g1[...] = d_u
    ng[...] = gain_term
    mean = jnp.zeros((ROWS, 128), F32)
    for j in range(8):
        d_branch = (g1[:, tile(j)] * valid[...]).astype(BF16)
        db[t, :, tile(j)] = d_branch
        mean = mean + d_branch.astype(F32) * total0[:, tile(j)]
    db_steps = spread_tokens(spreading, db, me)
    next(db_steps)
    mean = jnp.broadcast_to(jnp.sum(mean, axis=-1, keepdims=True), (128, 128))
    mean_row = jnp.transpose(mean)[0:8] / DI
    s = s0[0:1, :]
    row = iota((8, 128), 0)
    coef[t] = jnp.where(row == 0, s, jnp.where(row == 1, s * s * s * mean_row, 0.0))
    coef_copies = [small.send(coef.at[t], coef.at[t], peer) for peer in me.ts]
    next(layer1)
    next(db_steps)
    next(layer1)
    run(db_steps)
    for copy in coef_copies:
        copy.wait_recv()
    for link in (weights, tokens, small, spreading):
        link.drain()


def back_middle(*arrays):
    return pl.pallas_call(
        back_middle_kernel,
        out_shape=(
            jax.ShapeDtypeStruct((8, 768), F32),
            jax.ShapeDtypeStruct((8, 128), F32),
            jax.ShapeDtypeStruct((ROWS, D), F32),
            jax.ShapeDtypeStruct((1, D), F32),
            jax.ShapeDtypeStruct((4, ROWS, D), BF16),
            jax.ShapeDtypeStruct((4, 8, 128), F32),
            jax.ShapeDtypeStruct((4, 16, WALL), BF16),
            jax.ShapeDtypeStruct((4, 16, WALL), BF16),
        ),
        in_specs=[pl.BlockSpec(memory_space=pltpu.SMEM)] + vmem_specs(14),
        out_specs=tuple(vmem_specs(8)),
        scratch_shapes=bwd_scratch()[0] + bwd_scratch()[1] + token_scratch() + ring_scratch() + link_scratch(RING_COPIES, 6, 3, 6),
        compiler_params=pltpu.CompilerParams(
            collective_id=3, has_side_effects=True, vmem_limit_bytes=26 << 20
        ),
        name="backward_1_and_tokens",
    )(*arrays)


def small_sum(link, own, arrived, by_z, by_x, by_t, me):
    c, x, z, t = me.c, me.x, me.z, me.t
    swap = link.send(own.at[1 - c], arrived, me.core)
    yield
    swap.wait_recv()
    by_z[z] = own[c] + arrived[...]
    copies = [link.send(by_z.at[z], by_z.at[z], peer) for peer in me.zs]
    yield
    for copy in copies:
        copy.wait_recv()
    by_x[x] = by_z[0] + by_z[1] + by_z[2] + by_z[3]
    copies = [link.send(by_x.at[x], by_x.at[x], peer) for peer in me.xs]
    yield
    for copy in copies:
        copy.wait_recv()
    by_t[t] = by_x[0] + by_x[1] + by_x[2] + by_x[3]
    copies = [link.send(by_t.at[t], by_t.at[t], peer) for peer in me.ts]
    yield
    for copy in copies:
        copy.wait_recv()
    yield


def finish_kernel(
    lens, w0, proj0, kept0, yssd0, coef0, db0,
    part, u0, u1, g1, valid, par, coef1, ng1, sums1, heads1, sum_a1, sum_b1, hid0,
    lo, lg, smt, nmt, picked, o_bc,
    dh, d_proj0, scaled0, inn, xb, dyb, dyf, dx, bb, cb, d_c, cumr, colr, d_scaled0, sums0, heads0,
    relay, sums, inbox, relay2, sums2, inbox2, los, lgs, sms, smr, smz, smx, nms, nmr, nmz, nmx, sum_a0, sum_b0,
    grads, core_in, acc, g_relay, g_sums, g_inbox, w_grad0, bc_all0, last_in0, w_grad1, bc_all1, last_in1,
    g_s, g_r, f_s, f_r, l_s, l_r, p_s, p_r, q_s, q_r, b_s, b_r,
):
    me = Peers()
    c, x, z, t = me.c, me.x, me.z, me.t
    barrier_start(me.everyone())
    weights, final0, final1 = Link(g_s, g_r), Link(f_s, f_r), Link(l_s, l_r)
    tokens, tokens2, small = Link(p_s, p_r), Link(q_s, q_r), Link(b_s, b_r)
    last1 = reduce_last(final1, sum_a1, sum_b1, w_grad1, bc_all1, last_in1, me)
    out_steps = collect_tokens(tokens2, part, relay2, sums2, inbox2, me)

    def early():
        barrier_end(me.everyone())
        next(last1)
        next(out_steps)

    def later():
        next(last1)
        next(out_steps)

    mixer_bwd_kernel(
        0, lens, par, w0, proj0, kept0, yssd0, coef0, db0, dh, d_proj0, scaled0, sums0, heads0,
        inn, xb, dyb, dyf, dx, bb, cb, d_c, cumr, colr, d_scaled0, early=early, later=later,
    )
    for layer, (by_channel, heads) in enumerate(((sums0, heads0), (sums1, heads1))):
        sms[layer, 0:8, :] = by_channel[:, 0:512]
        sms[layer, 8:16, 0:256] = by_channel[:, 512:768]
        sms[layer, 8:16, 256:384] = heads[...]
        sms[layer, 8:16, 384:512] = jnp.zeros((8, 128), F32)
    chain = small_sum(small, sms, smr, smz, smx, smt, me)
    next(chain)
    back_steps = collect_tokens(tokens, dh, relay, sums, inbox, me)
    next(back_steps)
    layer0 = reduce_rings(
        weights, (hid0, d_proj0, db0, scaled0), grads, sum_a0, sum_b0, core_in, acc,
        g_relay, g_sums, g_inbox, me,
    )
    next(layer0)
    next(chain)
    next(back_steps)
    next(layer0)
    next(layer0)
    next(chain)
    los[0] = u1[...]
    lgs[1] = g1[...]
    run(back_steps)
    total = dh[t].astype(F32) + inbox[0].astype(F32) + inbox[1].astype(F32)
    d_u, gain_term = norm_back(u0[...], gain_of(par, 0), g1[...], total)
    lgs[0] = d_u
    lg_copy = small.send(lgs.at[1 - c], lg.at[c], me.core)
    lg[c] = lgs[c]
    next(layer0)
    for layer, term in enumerate((gain_term, ng1[...])):
        for j in range(8):
            nms[layer, j : j + 1, :] = term[:, tile(j)]
    norm_chain = small_sum(small, nms, nmr, nmz, nmx, nmt, me)
    next(norm_chain)
    next(chain)
    run(last1)
    next(norm_chain)
    next(layer0)
    last0 = reduce_last(final0, sum_a0, sum_b0, w_grad0, bc_all0, last_in0, me)
    next(last0)
    next(norm_chain)
    run(out_steps)
    los[1] = part[t].astype(F32) + inbox2[0].astype(F32) + inbox2[1].astype(F32)
    scale = column_of(coef1[t][0:1]) * valid[...]
    for j in range(8):
        los[1, :, tile(j)] = u1[:, tile(j)] + scale * los[1, :, tile(j)]
    lo_copy = small.send(los.at[1 - c], lo.at[c], me.core)
    lo[c] = los[c]
    next(norm_chain)
    next(last0)
    run(last0)
    picked[...] = jnp.where(c == 0, w_grad0[...], w_grad1[...])
    half = t // 2
    bc0 = bc_all0[0, half] + bc_all0[1, half] + bc_all0[2, half] + bc_all0[3, half]
    bc1 = bc_all1[0, half] + bc_all1[1, half] + bc_all1[2, half] + bc_all1[3, half]
    o_bc[...] = jnp.where(c == 0, bc0, bc1)
    run(chain)
    run(norm_chain)
    lo_copy.wait_recv()
    lg_copy.wait_recv()
    for link in (weights, final0, final1, tokens, tokens2, small):
        link.drain()


def finish(*arrays):
    return pl.pallas_call(
        finish_kernel,
        out_shape=(
            jax.ShapeDtypeStruct((2, ROWS, D), F32),
            jax.ShapeDtypeStruct((2, ROWS, D), F32),
            jax.ShapeDtypeStruct((4, 16, 512), F32),
            jax.ShapeDtypeStruct((4, 8, 128), F32),
            jax.ShapeDtypeStruct((64, WALL), F32),
            jax.ShapeDtypeStruct((16, 2 * N), F32),
        ),
        in_specs=[pl.BlockSpec(memory_space=pltpu.SMEM)] + vmem_specs(19),
        out_specs=tuple(vmem_specs(6)),
        scratch_shapes=bwd_scratch()[0] + bwd_scratch()[1]
        + [VM((T, CH), F32), VM((8, 768), F32), VM((8, 128), F32)]
        + token_scratch() + token_scratch()
        + [
            VM((2, ROWS, D), F32), VM((2, ROWS, D), F32),
            VM((2, 16, 512), F32), VM((16, 512), F32), VM((4, 16, 512), F32), VM((4, 16, 512), F32),
            VM((2, 8, 128), F32), VM((8, 128), F32), VM((4, 8, 128), F32), VM((4, 8, 128), F32),
            VM((4, 16, WALL), BF16), VM((4, 16, WALL), BF16),
        ]
        + ring_scratch() + last_scratch() + last_scratch()
        + link_scratch(RING_COPIES, LAST_COPIES, LAST_COPIES, 6, 6, 22),
        compiler_params=pltpu.CompilerParams(
            collective_id=4, has_side_effects=True, vmem_limit_bytes=34 << 20
        ),
        name="backward_0_and_gradients",
    )(*arrays)


def write_kernel(lo, lg, smt, nmt, picked, bc, *rest):
    outs, (in_part, dt, conv_w, conv_b, gain, norm, heads, sem) = rest[:13], rest[13:]
    (o_lo, o_lg, o_norm, o_in, o_bc, o_dt, o_cw, o_cb, o_dtb, o_alog, o_skip, o_gain, o_out) = outs
    copies = []

    def write(src, dst):
        copy = pltpu.make_async_copy(src, dst, sem.at[len(copies)])
        copy.start()
        copies.append(copy)

    write(lo, o_lo)
    write(lg, o_lg)
    write(bc, o_bc)
    in_part[:, 0, :] = picked[:, 0:512]
    in_part[:, 1, :] = picked[:, 512:1024]
    write(in_part, o_in)
    write(picked.at[:, pl.ds(WP, CH)], o_out)
    dt_rows = jnp.concatenate([picked[:, 1280:1408], jnp.zeros((64, 128), F32)], axis=0)
    dt[...] = jnp.transpose(dt_rows)[0:HL, 0:64]
    write(dt, o_dt)
    shared = smt[0, 8:16] + smt[1, 8:16] + smt[2, 8:16] + smt[3, 8:16]
    norms = nmt[0] + nmt[1] + nmt[2] + nmt[3]
    for j in range(8):
        norm[:, tile(j)] = norms[j : j + 1]
    write(norm, o_norm)
    conv_w[:, DI : DI + 2 * N] = shared[0:4, 0:256]
    conv_b[:, DI : DI + 2 * N] = shared[4:5, 0:256]
    for k in range(4):
        at = slice(512 * k, 512 * k + 512)
        conv_w[:, at] = smt[k, 0:4, :]
        conv_b[:, at] = smt[k, 4:5, :]
        gain[:, at] = smt[k, 5:6, :]
    write(conv_w, o_cw)
    write(conv_b, o_cb)
    write(gain, o_gain)
    all_heads = smt[0, 8:16, 256:384]
    for k in range(1, 4):
        all_heads = all_heads + pltpu.roll(smt[k, 8:16, 256:384], HL * k, 1)
    for k, out in ((0, o_dtb), (1, o_alog), (2, o_skip)):
        heads[k] = all_heads[k : k + 1, 0:H]
        write(heads.at[k], out)
    for copy in copies:
        copy.wait()


def write_outputs(*arrays):
    hbm_spec = pl.BlockSpec(memory_space=pltpu.HBM)
    shapes = [
        (2, ROWS, D), (2, ROWS, D), (1, D), (64, 2, CH), (16, 2 * N), (HL, 64), (CONV, DI + 2 * N),
        (1, DI + 2 * N), (1, H), (1, H), (1, H), (1, DI), (64, CH),
    ]
    return pl.pallas_call(
        write_kernel,
        out_shape=tuple(jax.ShapeDtypeStruct(shape, F32) for shape in shapes),
        in_specs=vmem_specs(6),
        out_specs=(hbm_spec,) * 13,
        scratch_shapes=[
            VM((64, 2, CH), F32), VM((HL, 64), F32), VM((CONV, DI + 2 * N), F32),
            VM((1, DI + 2 * N), F32), VM((1, DI), F32), VM((1, D), F32), VM((3, 1, H), F32),
            pltpu.SemaphoreType.DMA((13,)),
        ],
        compiler_params=pltpu.CompilerParams(vmem_limit_bytes=6 << 20),
        name="write_outputs",
    )(*arrays)


def body(
    activations, cotangent, lengths, norm_gain, in_weight, bc_weight, dt_weight, conv_weight,
    conv_bias, dt_bias, a_log, d_skip, gated_gain, out_weight,
):
    section = lax.axis_index("section")
    u0 = lax.dynamic_index_in_dim(activations, section, 0, keepdims=False)
    cot = lax.dynamic_index_in_dim(cotangent, section, 0, keepdims=False)
    flat = jnp.concatenate(
        [conv_bias, gated_gain, norm_gain, dt_bias, a_log, d_skip, jnp.zeros((1, 32), F32)], axis=1
    )
    w0, shard1, par, hid0, db1, valid = gather(
        lengths, in_weight[0].reshape(64, WZX), bc_weight[0], dt_weight[0].T, out_weight[0].T,
        conv_weight[0], flat, u0, cot,
    )
    proj0, kept0, y0, total0, u1, s0, hid1, w1 = middle(lengths, par, hid0, w0, u0, valid, shard1)
    proj1, kept1, part1, y1, coef1, d_scaled1 = mixer_fwd(1, lengths, par, hid1, w1, db1)
    sums1, heads1, g1, ng1, db0, coef0, sum_a1, sum_b1 = back_middle(
        lengths, par, w1, proj1, kept1, y1, coef1, d_scaled1, u1, cot, valid, total0, s0, hid1, db1
    )
    outs = write_outputs(
        *finish(
            lengths, w0, proj0, kept0, y0, coef0, db0, part1, u0, u1, g1, valid, par, coef1, ng1,
            sums1, heads1, sum_a1, sum_b1, hid0,
        )
    )
    outs = [out.T if k in (5, 12) else out for k, out in enumerate(outs)]
    plain = (2, 8, 9, 10, 7, 11)
    return tuple(out if k in plain else out[None] for k, out in enumerate(outs))


def solution(mesh):
    return jax.shard_map(
        body,
        mesh=mesh,
        in_specs=(
            P(None, ("dp", "tensor"), None),
            P(None, ("dp", "tensor"), None),
            P(None, "dp", None),
            P("section", None),
            P("section", "dp", None, "tensor"),
            P("section", "dp", None),
            P("section", "dp", "tensor"),
            P("section", None, None),
            P("section", None),
            P("section", None),
            P("section", None),
            P("section", None),
            P("section", None),
            P("section", "tensor", "dp"),
        ),
        out_specs=(
            P("section", None, ("dp", "tensor"), None),
            P("section", None, ("dp", "tensor"), None),
            P("section", None),
            P("section", "dp", None, "tensor"),
            P("section", ("dp", "tensor"), None),
            P("section", "dp", "tensor"),
            P("section", None, None),
            P("section", None),
            P("section", None),
            P("section", None),
            P("section", None),
            P("section", None),
            P("section", "tensor", "dp"),
        ),
        check_vma=False,
    )
```

profile of v0, /device:TPU:1, one launch (start us, length us, event | category | flops | bytes accessed | tf_op | source)
XLA Modules:
  0.0 156.7 jit_solution(4690596046321943467)
XLA Ops:
  0.6 0.0 copy-start.4
  0.7 0.8 concatenate.3.flat
  1.5 0.9 copy.27
  2.4 1.3 dynamic-slice_bitcast_fusion
  3.7 0.0 copy-start
  3.8 0.8 copy-done
  4.6 0.0 copy-start.1
  4.6 0.8 copy-done.1
  5.4 0.0 copy-start.2
  5.4 0.8 copy-done.2
  6.1 0.0 copy-start.3
  6.1 0.7 copy-done.3
  6.8 0.0 copy-start.5
  6.8 0.7 copy-done.5
  7.5 29.2 %gather_weights.1 = (bf16[4,4,64,1920]{3,2,1,0:T(8,128)(2,1)S(1)}, bf16[32,1920]{1,0:T(8,128)(2,1)S(1)}, f32[2,8,2432]{2,1,0:T(8,128)S(1)}, bf16[4,128,1024]{2,1...) custom-call(s32[2,1,2]{2,1,0:T(1,128)S(1)} %copy-done.3, bf16[64,1024]{1,0:T(8,128)(2,1)S(1)} %bitcast.26, ...), custom_call_target="tpu_custom_call" | custom-call | tf_op jit(solution)/shard_map/gather_weights/pallas_call | solution.py:771
  36.7 0.0 copy-done.4
  36.7 28.5 %forward_0_and_tokens.1 = (f32[512,1408]{1,0:T(8,128)S(1)}, f32[512,768]{1,0:T(8,128)S(1)}, f32[512,512]{1,0:T(8,128)S(1)}, f32[128,1024]{1,0:T(8,128)S(1)}, f32...) custom-call(s32[2,1,2]{2,1,0:T(1,128)S(1)} %copy-done.4, ...), custom_call_target="tpu_custom_call" | custom-call | tf_op jit(solution)/shard_map/forward_0_and_tokens/pallas_call | solution.py:847
  65.2 8.9 %mixer_fwd.1 = (f32[512,1408]{1,0:T(8,128)S(1)}, f32[512,768]{1,0:T(8,128)S(1)}, bf16[4,128,1024]{2,1,0:T(8,128)(2,1)S(1)}, f32[512,512]{1,0:T(8,128)S(1)}, f32[...) custom-call(s32[2,1,2]{2,1,0:T(1,128)S(1)} %copy-done.4, f32[2,8,2432]{2,1,0:T(8,128)S(1)} %get-tuple-element.61.par, ...), custom_call_target="tpu_custom_call" | custom-call | tf_op jit(solution)/shard_map/mixer_fwd/pallas_call | solution.py:248
  74.1 34.7 %backward_1_and_tokens.1 = (f32[8,768]{1,0:T(8,128)S(1)}, f32[8,128]{1,0:T(8,128)S(1)}, f32[128,1024]{1,0:T(8,128)S(1)}, f32[1,1024]{1,0:T(1,128)S(1)}, bf16[4,1...) custom-call(s32[2,1,2]{2,1,0:T(1,128)S(1)} %copy-done.4, ...), custom_call_target="tpu_custom_call" | custom-call | tf_op jit(solution)/shard_map/backward_1_and_tokens/pallas_call | solution.py:950
  108.8 46.1 %backward_0_and_gradients.1 = (f32[2,128,1024]{2,1,0:T(8,128)S(1)}, f32[2,128,1024]{2,1,0:T(8,128)S(1)}, f32[4,16,512]{2,1,0:T(8,128)S(1)}, f32[4,8,128]{2,1,0:T...) custom-call(s32[2,1,2]{2,1,0:T(1,128)S(1)} %copy-done.4, bf16[4,4,64,1920]{3,2,1,0:T(8,128)(2,1)S(1)} %get-tuple-element.60.w0, ...), custom_call_target="tpu_custom_call" | custom-call | tf_op jit(solution)/shard_map/backward_0_and_gradients/pallas_call | solution.py:1089
  154.9 1.6 %write_outputs.1 = (f32[2,128,1024]{2,1,0:T(8,128)}, f32[2,128,1024]{2,1,0:T(8,128)}, f32[1,1024]{1,0:T(1,128)}, f32[64,2,512]{2,1,0:T(2,128)}, f32[16,256]{1,0:...) custom-call(f32[2,128,1024]{2,1,0:T(8,128)S(1)} %get-tuple-element.8, ...), custom_call_target="tpu_custom_call" | custom-call | tf_op jit(solution)/shard_map/write_outputs/pallas_call | solution.py:1170
  (1 shorter events, 0.0 us)
Async XLA Ops:
  0.6 36.0 %copy-start.4 = (s32[2,1,2]{2,1,0:T(1,128)S(1)}, s32[2,1,2]{2,1,0:T(1,128)}, u32[]{:S(2)}) copy-start(s32[2,1,2]{2,1,0:T(1,128)} %lens.7) | copy-start | bytes 52
  3.7 0.8 copy-start
  4.6 0.8 copy-start.1
  5.4 0.8 copy-start.2
  6.1 0.7 copy-start.3
  6.8 0.7 copy-start.5
where the time goes:
time: 160 us; the launch traced here: 157 us
  Pallas kernels  149 us (93%)
  local copies, waits for them, and re-layouts  6.79 us (4%)
    pallas_call x1, Pallas kernels, finish(): pl.pallas_call(finish_kernel, out_shape=(jax.ShapeDtypeStruct((2, ROWS, D...  46.1 us
    pallas_call x1, Pallas kernels, back_middle(): pl.pallas_call(back_middle_kernel, out_shape=(jax.ShapeDtypeStruct((8, 76...  34.7 us
    pallas_call x1, Pallas kernels, gather(): pl.pallas_call(gather_kernel, out_shape=(jax.ShapeDtypeStruct((4, 4, 64,...  29.2 us
    pallas_call x1, Pallas kernels, middle(): pl.pallas_call(middle_kernel, out_shape=(jax.ShapeDtypeStruct((T, WP), F3...  28.5 us
    pallas_call x1, Pallas kernels, mixer_fwd(): pl.pallas_call(functools.partial(mixer_fwd_kernel, layer), out_shape=tupl...  8.91 us
    unnamed x13, local copies, waits for them, and re-layouts  4.65 us

commit v1 on v0

--- a/solution.py
+++ b/solution.py
@@ -1043,13 +1043,13 @@
     next(chain)
     los[0] = u1[...]
     lgs[1] = g1[...]
+    next(layer0)
     run(back_steps)
     total = dh[t].astype(F32) + inbox[0].astype(F32) + inbox[1].astype(F32)
     d_u, gain_term = norm_back(u0[...], gain_of(par, 0), g1[...], total)
     lgs[0] = d_u
     lg_copy = small.send(lgs.at[1 - c], lg.at[c], me.core)
     lg[c] = lgs[c]
-    next(layer0)
     for layer, term in enumerate((gain_term, ng1[...])):
         for j in range(8):
             nms[layer, j : j + 1, :] = term[:, tile(j)]

time: 160 us -> 160 us (level)
  no operation moved by 1% of the time
where the time goes in v1:
time: 160 us; the launch traced here: 157 us
  Pallas kernels  149 us (93%)
  local copies, waits for them, and re-layouts  6.79 us (4%)
    pallas_call x1, Pallas kernels, finish(): pl.pallas_call(finish_kernel, out_shape=(jax.ShapeDtypeStruct((2, ROWS, D...  46.1 us
    pallas_call x1, Pallas kernels, back_middle(): pl.pallas_call(back_middle_kernel, out_shape=(jax.ShapeDtypeStruct((8, 76...  34.7 us
    pallas_call x1, Pallas kernels, gather(): pl.pallas_call(gather_kernel, out_shape=(jax.ShapeDtypeStruct((4, 4, 64,...  29.2 us
    pallas_call x1, Pallas kernels, middle(): pl.pallas_call(middle_kernel, out_shape=(jax.ShapeDtypeStruct((T, WP), F3...  28.5 us
    pallas_call x1, Pallas kernels, mixer_fwd(): pl.pallas_call(functools.partial(mixer_fwd_kernel, layer), out_shape=tupl...  8.91 us
    unnamed x13, local copies, waits for them, and re-layouts  4.65 us

profile of v1, /device:TPU:1, one launch (start us, length us, event | category | flops | bytes accessed | tf_op | source)
XLA Modules:
  0.0 156.7 jit_solution(16139630092839827347)
XLA Ops:
  0.6 0.0 copy-start.4
  0.7 0.8 concatenate.3.flat
  1.5 0.9 copy.27
  2.4 1.3 dynamic-slice_bitcast_fusion
  3.7 0.0 copy-start
  3.8 0.8 copy-done
  4.6 0.0 copy-start.1
  4.6 0.8 copy-done.1
  5.4 0.0 copy-start.2
  5.4 0.8 copy-done.2
  6.1 0.0 copy-start.3
  6.1 0.7 copy-done.3
  6.8 0.0 copy-start.5
  6.8 0.7 copy-done.5
  7.5 29.2 %gather_weights.1 = (bf16[4,4,64,1920]{3,2,1,0:T(8,128)(2,1)S(1)}, bf16[32,1920]{1,0:T(8,128)(2,1)S(1)}, f32[2,8,2432]{2,1,0:T(8,128)S(1)}, bf16[4,128,1024]{2,1...) custom-call(s32[2,1,2]{2,1,0:T(1,128)S(1)} %copy-done.3, bf16[64,1024]{1,0:T(8,128)(2,1)S(1)} %bitcast.26, ...), custom_call_target="tpu_custom_call" | custom-call | tf_op jit(solution)/shard_map/gather_weights/pallas_call | solution.py:771
  36.7 0.0 copy-done.4
  36.7 28.5 %forward_0_and_tokens.1 = (f32[512,1408]{1,0:T(8,128)S(1)}, f32[512,768]{1,0:T(8,128)S(1)}, f32[512,512]{1,0:T(8,128)S(1)}, f32[128,1024]{1,0:T(8,128)S(1)}, f32...) custom-call(s32[2,1,2]{2,1,0:T(1,128)S(1)} %copy-done.4, ...), custom_call_target="tpu_custom_call" | custom-call | tf_op jit(solution)/shard_map/forward_0_and_tokens/pallas_call | solution.py:847
  65.2 8.9 %mixer_fwd.1 = (f32[512,1408]{1,0:T(8,128)S(1)}, f32[512,768]{1,0:T(8,128)S(1)}, bf16[4,128,1024]{2,1,0:T(8,128)(2,1)S(1)}, f32[512,512]{1,0:T(8,128)S(1)}, f32[...) custom-call(s32[2,1,2]{2,1,0:T(1,128)S(1)} %copy-done.4, f32[2,8,2432]{2,1,0:T(8,128)S(1)} %get-tuple-element.61.par, ...), custom_call_target="tpu_custom_call" | custom-call | tf_op jit(solution)/shard_map/mixer_fwd/pallas_call | solution.py:248
  74.1 34.7 %backward_1_and_tokens.1 = (f32[8,768]{1,0:T(8,128)S(1)}, f32[8,128]{1,0:T(8,128)S(1)}, f32[128,1024]{1,0:T(8,128)S(1)}, f32[1,1024]{1,0:T(1,128)S(1)}, bf16[4,1...) custom-call(s32[2,1,2]{2,1,0:T(1,128)S(1)} %copy-done.4, ...), custom_call_target="tpu_custom_call" | custom-call | tf_op jit(solution)/shard_map/backward_1_and_tokens/pallas_call | solution.py:950
  108.8 46.1 %backward_0_and_gradients.1 = (f32[2,128,1024]{2,1,0:T(8,128)S(1)}, f32[2,128,1024]{2,1,0:T(8,128)S(1)}, f32[4,16,512]{2,1,0:T(8,128)S(1)}, f32[4,8,128]{2,1,0:T...) custom-call(s32[2,1,2]{2,1,0:T(1,128)S(1)} %copy-done.4, bf16[4,4,64,1920]{3,2,1,0:T(8,128)(2,1)S(1)} %get-tuple-element.60.w0, ...), custom_call_target="tpu_custom_call" | custom-call | tf_op jit(solution)/shard_map/backward_0_and_gradients/pallas_call | solution.py:1089
  154.9 1.6 %write_outputs.1 = (f32[2,128,1024]{2,1,0:T(8,128)}, f32[2,128,1024]{2,1,0:T(8,128)}, f32[1,1024]{1,0:T(1,128)}, f32[64,2,512]{2,1,0:T(2,128)}, f32[16,256]{1,0:...) custom-call(f32[2,128,1024]{2,1,0:T(8,128)S(1)} %get-tuple-element.8, ...), custom_call_target="tpu_custom_call" | custom-call | tf_op jit(solution)/shard_map/write_outputs/pallas_call | solution.py:1170
  (1 shorter events, 0.0 us)
Async XLA Ops:
  0.6 36.0 %copy-start.4 = (s32[2,1,2]{2,1,0:T(1,128)S(1)}, s32[2,1,2]{2,1,0:T(1,128)}, u32[]{:S(2)}) copy-start(s32[2,1,2]{2,1,0:T(1,128)} %lens.7) | copy-start | bytes 52
  3.7 0.8 copy-start
  4.6 0.8 copy-start.1
  5.4 0.8 copy-start.2
  6.1 0.7 copy-start.3
  6.8 0.7 copy-start.5

commit v2 on v1

--- a/solution.py
+++ b/solution.py
@@ -1055,12 +1055,12 @@
             nms[layer, j : j + 1, :] = term[:, tile(j)]
     norm_chain = small_sum(small, nms, nmr, nmz, nmx, nmt, me)
     next(norm_chain)
+    next(layer0)
+    last0 = reduce_last(final0, sum_a0, sum_b0, w_grad0, bc_all0, last_in0, me)
+    next(last0)
     next(chain)
     run(last1)
     next(norm_chain)
-    next(layer0)
-    last0 = reduce_last(final0, sum_a0, sum_b0, w_grad0, bc_all0, last_in0, me)
-    next(last0)
     next(norm_chain)
     run(out_steps)
     los[1] = part[t].astype(F32) + inbox2[0].astype(F32) + inbox2[1].astype(F32)
@@ -1069,8 +1069,8 @@
         los[1, :, tile(j)] = u1[:, tile(j)] + scale * los[1, :, tile(j)]
     lo_copy = small.send(los.at[1 - c], lo.at[c], me.core)
     lo[c] = los[c]
+    next(last0)
     next(norm_chain)
-    next(last0)
     run(last0)
     picked[...] = jnp.where(c == 0, w_grad0[...], w_grad1[...])
     half = t // 2

time: 160 us -> 161 us (level)
  the two profiles are of different devices: /device:TPU:1 before, /device:TPU:0 now
where the time goes in v2:
time: 161 us; the launch traced here: 159 us
  Pallas kernels  151 us (94%)
  local copies, waits for them, and re-layouts  6.79 us (4%)
    pallas_call x1, Pallas kernels, finish(): pl.pallas_call(finish_kernel, out_shape=(jax.ShapeDtypeStruct((2, ROWS, D...  48.3 us
    pallas_call x1, Pallas kernels, back_middle(): pl.pallas_call(back_middle_kernel, out_shape=(jax.ShapeDtypeStruct((8, 76...  32.4 us
    pallas_call x1, Pallas kernels, middle(): pl.pallas_call(middle_kernel, out_shape=(jax.ShapeDtypeStruct((T, WP), F3...  29.8 us
    pallas_call x1, Pallas kernels, gather(): pl.pallas_call(gather_kernel, out_shape=(jax.ShapeDtypeStruct((4, 4, 64,...  28.5 us
    pallas_call x1, Pallas kernels, mixer_fwd(): pl.pallas_call(functools.partial(mixer_fwd_kernel, layer), out_shape=tupl...  10.3 us
    unnamed x13, local copies, waits for them, and re-layouts  4.65 us

profile of v2, /device:TPU:0, one launch (start us, length us, event | category | flops | bytes accessed | tf_op | source)
XLA Modules:
  0.0 158.5 jit_solution(13769307732058853355)
XLA Ops:
  0.6 0.0 copy-start.4
  0.7 0.8 concatenate.3.flat
  1.5 0.9 copy.27
  2.4 1.3 dynamic-slice_bitcast_fusion
  3.7 0.0 copy-start
  3.8 0.8 copy-done
  4.6 0.0 copy-start.1
  4.6 0.8 copy-done.1
  5.4 0.0 copy-start.2
  5.4 0.8 copy-done.2
  6.1 0.0 copy-start.3
  6.1 0.7 copy-done.3
  6.8 0.0 copy-start.5
  6.8 0.7 copy-done.5
  7.5 28.5 %gather_weights.1 = (bf16[4,4,64,1920]{3,2,1,0:T(8,128)(2,1)S(1)}, bf16[32,1920]{1,0:T(8,128)(2,1)S(1)}, f32[2,8,2432]{2,1,0:T(8,128)S(1)}, bf16[4,128,1024]{2,1...) custom-call(s32[2,1,2]{2,1,0:T(1,128)S(1)} %copy-done.3, bf16[64,1024]{1,0:T(8,128)(2,1)S(1)} %bitcast.26, ...), custom_call_target="tpu_custom_call" | custom-call | tf_op jit(solution)/shard_map/gather_weights/pallas_call | solution.py:771
  35.9 0.0 copy-done.4
  35.9 29.8 %forward_0_and_tokens.1 = (f32[512,1408]{1,0:T(8,128)S(1)}, f32[512,768]{1,0:T(8,128)S(1)}, f32[512,512]{1,0:T(8,128)S(1)}, f32[128,1024]{1,0:T(8,128)S(1)}, f32...) custom-call(s32[2,1,2]{2,1,0:T(1,128)S(1)} %copy-done.4, ...), custom_call_target="tpu_custom_call" | custom-call | tf_op jit(solution)/shard_map/forward_0_and_tokens/pallas_call | solution.py:847
  65.7 10.3 %mixer_fwd.1 = (f32[512,1408]{1,0:T(8,128)S(1)}, f32[512,768]{1,0:T(8,128)S(1)}, bf16[4,128,1024]{2,1,0:T(8,128)(2,1)S(1)}, f32[512,512]{1,0:T(8,128)S(1)}, f32[...) custom-call(s32[2,1,2]{2,1,0:T(1,128)S(1)} %copy-done.4, f32[2,8,2432]{2,1,0:T(8,128)S(1)} %get-tuple-element.61.par, ...), custom_call_target="tpu_custom_call" | custom-call | tf_op jit(solution)/shard_map/mixer_fwd/pallas_call | solution.py:248
  76.0 32.4 %backward_1_and_tokens.1 = (f32[8,768]{1,0:T(8,128)S(1)}, f32[8,128]{1,0:T(8,128)S(1)}, f32[128,1024]{1,0:T(8,128)S(1)}, f32[1,1024]{1,0:T(1,128)S(1)}, bf16[4,1...) custom-call(s32[2,1,2]{2,1,0:T(1,128)S(1)} %copy-done.4, ...), custom_call_target="tpu_custom_call" | custom-call | tf_op jit(solution)/shard_map/backward_1_and_tokens/pallas_call | solution.py:950
  108.4 48.3 %backward_0_and_gradients.1 = (f32[2,128,1024]{2,1,0:T(8,128)S(1)}, f32[2,128,1024]{2,1,0:T(8,128)S(1)}, f32[4,16,512]{2,1,0:T(8,128)S(1)}, f32[4,8,128]{2,1,0:T...) custom-call(s32[2,1,2]{2,1,0:T(1,128)S(1)} %copy-done.4, bf16[4,4,64,1920]{3,2,1,0:T(8,128)(2,1)S(1)} %get-tuple-element.60.w0, ...), custom_call_target="tpu_custom_call" | custom-call | tf_op jit(solution)/shard_map/backward_0_and_gradients/pallas_call | solution.py:1089
  156.7 1.6 write_outputs.1
  (1 shorter events, 0.0 us)
Async XLA Ops:
  0.6 35.3 %copy-start.4 = (s32[2,1,2]{2,1,0:T(1,128)S(1)}, s32[2,1,2]{2,1,0:T(1,128)}, u32[]{:S(2)}) copy-start(s32[2,1,2]{2,1,0:T(1,128)} %lens.7) | copy-start | bytes 52
  3.7 0.8 copy-start
  4.6 0.8 copy-start.1
  5.4 0.8 copy-start.2
  6.1 0.7 copy-start.3
  6.8 0.7 copy-start.5
